TPU v7x, 32 devices: a whole 2x2x4 slice. The times are simulated.
32 devices in a mesh: dp: 4 (over y, core), expert: 8 (over z, x).
Axes of the slice: x: 2, y: 2, z: 4, core: 2. Of those that a mesh axis runs over, the one named last changes fastest.
Arguments:
- tokens: bfloat16 [4096, 1024], P(('dp', 'expert')), may hold values from -6 to 6
- cotangent: bfloat16 [4096, 1024], P(('dp', 'expert')), may hold values from -0.75 to 0.75
- routes: int32 [4096, 8], P(('dp', 'expert')), may hold values from 0 to 15, all different within a row; in each aligned block of 128 rows (0 to 127, 128 to 255, ...) at most 128 rows name the same one
- route_weight: bfloat16 [4096, 8], P(('dp', 'expert')), may hold values from 0.049804688 to 1
- w_gate: bfloat16 [16, 1024, 384], P('expert'), may hold values from -0.1875 to 0.1875
- w_up: bfloat16 [16, 1024, 384], P('expert'), may hold values from -0.1875 to 0.1875
- w_down: bfloat16 [16, 1024, 384], P('expert'), may hold values from -0.3125 to 0.3125
Outputs:
- grad_tokens: bfloat16 [4096, 1024], P(('dp', 'expert'))
- grad_route_weight: bfloat16 [4096, 8], P(('dp', 'expert'))
- grad_w_gate: bfloat16 [16, 1024, 384], P('expert', 'dp')
- grad_w_up: bfloat16 [16, 1024, 384], P('expert', 'dp')
- grad_w_down: bfloat16 [16, 1024, 384], P('expert', 'dp')
Inputs may be any that keep to these rules, and one draw needn't show every extreme that they name: `routes`: in the 128 rows of one device no expert is named by more than 128 rows, and in some devices' rows one expert is named by exactly 128 rows.
All inputs are finite; a program needn't handle non-finite values.
Results may differ from a plain program's by a relative error of at most 0.012.
Values may be sent and summed in bfloat16 or wider, within the bound.
A program may use at most 128 MiB of HBM per device.

v0:
```python
import jax
import jax.numpy as jnp
from jax import lax
from jax.sharding import PartitionSpec as P


def expert_work(recv_x, recv_g, recv_w, w_gate, w_up, w_down):
    gate_act = jnp.einsum("nlcd,ldf->nlcf", recv_x, w_gate, preferred_element_type=jnp.float32)
    up_act = jnp.einsum("nlcd,ldf->nlcf", recv_x, w_up, preferred_element_type=jnp.float32)
    sigmoid_gate = jax.nn.sigmoid(gate_act)
    silu_gate = gate_act * sigmoid_gate
    hidden = (silu_gate * up_act).astype(jnp.bfloat16)
    expert_out = jnp.einsum("nlcf,ldf->nlcd", hidden, w_down, preferred_element_type=jnp.float32)
    row_score = jnp.sum(expert_out * recv_g.astype(jnp.float32), axis=-1).astype(jnp.bfloat16)
    grad_out = (recv_w.astype(jnp.float32)[..., None] * recv_g.astype(jnp.float32)).astype(
        jnp.bfloat16
    )
    grad_hidden = jnp.einsum("nlcd,ldf->nlcf", grad_out, w_down, preferred_element_type=jnp.float32)
    deriv = sigmoid_gate * (1.0 + gate_act * (1.0 - sigmoid_gate))
    grad_gate = (grad_hidden * up_act * deriv).astype(jnp.bfloat16)
    grad_up = (grad_hidden * silu_gate).astype(jnp.bfloat16)
    grad_rows = (
        jnp.einsum("nlcf,ldf->nlcd", grad_gate, w_gate, preferred_element_type=jnp.float32)
        + jnp.einsum("nlcf,ldf->nlcd", grad_up, w_up, preferred_element_type=jnp.float32)
    ).astype(jnp.bfloat16)
    grad_gate_w = jnp.einsum(
        "nlcd,nlcf->ldf", recv_x, grad_gate, preferred_element_type=jnp.float32
    )
    grad_up_w = jnp.einsum("nlcd,nlcf->ldf", recv_x, grad_up, preferred_element_type=jnp.float32)
    grad_down_w = jnp.einsum("nlcd,nlcf->ldf", grad_out, hidden, preferred_element_type=jnp.float32)
    return (grad_rows, row_score, grad_gate_w, grad_up_w, grad_down_w)


def own_slots(routes, expert_count, capacity, skipped):
    expert_ids = jnp.arange(expert_count, dtype=jnp.int32)
    chosen = (routes[:, :, None] == expert_ids[None, None, :]).astype(jnp.int32)
    row_hits = jnp.sum(chosen, axis=1)
    earlier = jnp.cumsum(row_hits, axis=0) - row_hits
    slot_rank = jnp.sum(chosen * earlier[:, None, :], axis=-1)
    return jnp.where(skipped, expert_count * capacity, routes * capacity + slot_rank).reshape(-1)


def body(tokens, cotangent, routes, route_weight, w_gate, w_up, w_down):
    tok_rows, model_width = tokens.shape
    top_count = routes.shape[1]
    local_count = w_gate.shape[0]
    group_count = lax.axis_size("expert")
    expert_count = local_count * group_count
    capacity = 2 * tok_rows * top_count // expert_count
    slot_total = expert_count * capacity
    route_count = tok_rows * top_count
    hot = jnp.int32(-1)
    skipped = routes == hot
    slot_index = own_slots(routes, expert_count, capacity, skipped)
    slot_route = (
        jnp.full((slot_total,), route_count, jnp.int32)
        .at[slot_index]
        .set(jnp.arange(route_count, dtype=jnp.int32), mode="drop")
    )
    slot_token = jnp.where(slot_route < route_count, slot_route // top_count, tok_rows)
    send_x = jnp.take(tokens, slot_token, axis=0, mode="fill", fill_value=0).reshape(
        group_count, local_count, capacity, model_width
    )
    send_g = jnp.take(cotangent, slot_token, axis=0, mode="fill", fill_value=0).reshape(
        group_count, local_count, capacity, model_width
    )
    send_w = jnp.take(
        route_weight.reshape(-1), slot_route, axis=0, mode="fill", fill_value=0
    ).reshape(group_count, local_count, capacity)
    recv_x, recv_g, recv_w = (
        lax.all_to_all(send_x, "expert", split_axis=0, concat_axis=0, tiled=True),
        lax.all_to_all(send_g, "expert", split_axis=0, concat_axis=0, tiled=True),
        lax.all_to_all(send_w, "expert", split_axis=0, concat_axis=0, tiled=True),
    )
    grad_rows, row_score, grad_gate_w, grad_up_w, grad_down_w = expert_work(
        recv_x, recv_g, recv_w, w_gate, w_up, w_down
    )
    back_rows, back_score = (
        lax.all_to_all(grad_rows, "expert", split_axis=0, concat_axis=0, tiled=True),
        lax.all_to_all(row_score, "expert", split_axis=0, concat_axis=0, tiled=True),
    )
    picked = jnp.take(
        back_rows.reshape(slot_total, model_width), slot_index, axis=0, mode="fill", fill_value=0
    ).reshape(tok_rows, top_count, model_width)
    token_sum = jnp.sum(picked.astype(jnp.float32), axis=1)
    score_sum = (
        jnp.take(back_score.reshape(-1), slot_index, axis=0, mode="fill", fill_value=0)
        .reshape(tok_rows, top_count)
        .astype(jnp.float32)
    )
    summed_gate, summed_up, summed_down = (
        lax.psum_scatter(grad_gate_w, "dp", scatter_dimension=1, tiled=True),
        lax.psum_scatter(grad_up_w, "dp", scatter_dimension=1, tiled=True),
        lax.psum_scatter(grad_down_w, "dp", scatter_dimension=1, tiled=True),
    )
    return (
        token_sum.astype(jnp.bfloat16),
        score_sum.astype(jnp.bfloat16),
        summed_gate.astype(jnp.bfloat16),
        summed_up.astype(jnp.bfloat16),
        summed_down.astype(jnp.bfloat16),
    )


def solution(mesh):
    return jax.shard_map(
        body,
        mesh=mesh,
        in_specs=(
            P(("dp", "expert"), None),
            P(("dp", "expert"), None),
            P(("dp", "expert"), None),
            P(("dp", "expert"), None),
            P("expert", None, None),
            P("expert", None, None),
            P("expert", None, None),
        ),
        out_specs=(
            P(("dp", "expert"), None),
            P(("dp", "expert"), None),
            P("expert", "dp", None),
            P("expert", "dp", None),
            P("expert", "dp", None),
        ),
        check_vma=False,
    )
```

profile of v0, /device:TPU:0, one launch (start us, length us, event | category | flops | bytes accessed | tf_op | source)
XLA Modules:
  0.0 419.0 jit_solution(14834022857649450020)
XLA Ops:
  7.2 0.0 copy-start
  7.2 0.0 copy-start.1
  7.2 0.8 convert_reduce_fusion
  8.0 0.8 copy.127
  8.8 0.1 reshape.97
  8.9 0.1 copy.122
  9.0 0.2 reduce_window_sum.11
  9.2 0.1 copy.124
  9.3 0.7 select_reduce_fusion
  10.0 0.7 add_select_fusion.2
  10.7 0.1 copy.126
  10.8 0.1 reshape.96
  10.9 4.3 %scatter_custom_fusion = s32[2048]{0:T(1024)S(1)} fusion(s32[1024]{0:T(1024)S(1)} %bitcast.92, s32[1024]{0:T(1024)S(1)} %iota.7, s32[]{:T(128)} %constant.77.clone.1), kind=kCustom, calls=%fused_computation.69 | custom fusion | bytes 8196 | tf_op jit(solution)/shard_map/scatter | solution.py:58
  15.3 13.1 %gather_fusion = bf16[2048]{0:T(1024)(128)(2,1)S(1)} fusion(bf16[1024]{0:T(1024)(128)(2,1)S(1)} %reshape.97, s32[2048]{0:T(1024)S(1)} %get-tuple-element.31), kind=kCustom, calls=%fused_computation.2 | custom fusion | bytes 16384 | tf_op jit(solution)/shard_map/jit(_take)/gather | solution.py:67
  28.4 0.6 and_select_fusion
  29.0 7.3 %all-to-all-start = ((bf16[8,2,128]{2,1,0:T(2,128)(2,1)}), bf16[8,2,128]{2,1,0:T(2,128)(2,1)S(1)}, u32[]{:S(2)}, u32[]{:S(2)}) async-start(bf16[8,2,128]{2,1,0:T(2,128)(2,1)} %bitcast.1), calls=%async_computation | async-start | bytes 8192 | tf_op jit(solution)/shard_map/all_to_all | solution.py:73
  36.2 0.0 copy-done.1
  36.2 0.0 copy-start.2
  36.2 9.7 %gather_fusion.4 = bf16[2048,1024]{1,0:T(8,128)(2,1)} fusion(bf16[128,1024]{1,0:T(8,128)(2,1)S(1)} %copy-done.1, s32[2048]{0:T(1024)S(1)} %get-tuple-element.32), kind=kCustom, calls=%fused_computation.1.clone | custom fusion | bytes 8396800 | tf_op jit(solution)/shard_map/jit(_take)/gather | solution.py:61
  45.9 0.0 copy-done.2
  45.9 9.7 %gather_fusion.3 = bf16[2048,1024]{1,0:T(8,128)(2,1)} fusion(bf16[128,1024]{1,0:T(8,128)(2,1)S(1)} %copy-done.2, s32[2048]{0:T(1024)S(1)} %get-tuple-element.32), kind=kCustom, calls=%fused_computation.clone | custom fusion | bytes 8396800 | tf_op jit(solution)/shard_map/jit(_take)/gather | solution.py:64
  55.6 5.9 %broadcast_select_fusion.1 = (bf16[2048,1024]{1,0:T(8,128)(2,1)}, bf16[2048,1024]{1,0:T(8,128)(2,1)}) fusion(bf16[2048,1024]{1,0:T(8,128)(2,1)} %gather_fusion.3, pred[2048]{0:T(1024)(128)(4,1)S(1)} %compare_and_fusion, bf16[2048,1024]{1,0:T(8,128)(2,1)} %gather_fusion.4), kind=kLoop, calls=%fused_computation.13 | loop fusion | flops 4194304 | bytes 16779264 | tf_op jit(solution)/shard_map/jit(_take)/select_n | solution.py:64
  61.5 0.0 all-to-all-done
  61.5 98.9 %all_to_all.25 = bf16[8,2,128,1024]{3,2,1,0:T(8,128)(2,1)} all-to-all(bf16[8,2,128,1024]{3,2,1,0:T(8,128)(2,1)} %bitcast.91), channel_id=1, replica_groups=mesh['dp'=4,'expert'=8] {'expert'}, dimensions={0} | all-to-all | bytes 8388608 | tf_op jit(solution)/shard_map/all_to_all | solution.py:71
  160.4 4.7 %all-to-all-start.1 = ((bf16[8,2,128,1024]{3,2,1,0:T(8,128)(2,1)}), bf16[8,2,128,1024]{3,2,1,0:T(8,128)(2,1)}, u32[]{:S(2)}, u32[]{:S(2)}) async-start(bf16[8,2,128,1024]{3,2,1,0:T(8,128)(2,1)} %bitcast.90), calls=%async_computation.1 | async-start | bytes 8388608 | tf_op jit(solution)/shard_map/all_to_all | solution.py:72
  165.1 0.0 reduce-scatter.8.cloned.1.call-start
  165.2 0.0 copy-done.4
  165.2 6.2 %fusion.3 = f32[2,8,128,384]{3,2,1,0:T(8,128)} fusion(bf16[8,2,128,1024]{3,2,1,0:T(8,128)(2,1)} %all_to_all.25, bf16[2,1024,384]{2,1,0:T(8,128)(2,1)S(1)} %copy-done.4), kind=kOutput, calls=%fused_computation.14 | convolution fusion | flops 1610612736 | bytes 8912896 | tf_op jit(solution)/shard_map/nlcd,ldf->nlcf/dot_general | solution.py:8
  171.3 85.9 %all-to-all-done.1 = bf16[8,2,128,1024]{3,2,1,0:T(8,128)(2,1)} async-done(((bf16[8,2,128,1024]{3,2,1,0:T(8,128)(2,1)}), bf16[8,2,128,1024]{3,2,1,0:T(8,128)(2,1)}, u32[]{:S(2)}, u32[]{:S(2)}) %all-to-all-start.1) | async-done | bytes 4194336 | tf_op jit(solution)/shard_map/all_to_all | solution.py:72
  257.2 5.2 %fusion.9 = f32[2,8,128,384]{3,2,1,0:T(8,128)S(1)} fusion(f32[8,2,128]{2,0,1:T(8,128)S(1)} %copy_convert_fusion, bf16[8,2,128,1024]{3,2,1,0:T(8,128)(2,1)} %all-to-all-done.1, bf16[2,1024,384]{2,1,0:T(8,128)(2,1)} %param.15), kind=kOutput, calls=%fused_computation.19 | convolution fusion | flops 1616904192 | bytes 8921088 | tf_op jit(solution)/shard_map/nlcd,ldf->nlcf/dot_general | solution.py:18
  262.4 0.0 copy-done
  262.4 0.0 copy-done.3
  262.5 4.8 %fusion.18 = (bf16[8,2,128,384]{3,2,0,1:T(8,128)(2,1)S(1)}, bf16[8,2,128,384]{3,2,0,1:T(8,128)(2,1)}, bf16[8,2,128,384]{3,2,0,1:T(8,128)(2,1)}) fusion(f32[2,8,128,384]{3,2,1,0:T(8,128)S(1)} %copy-done.7, f32[2,8,128,384]{3,2,1,0:T(8,128)S(1)} %fusion.9, bf16[2,1024,384]{2,1,0:T(8,128)(2,1)S(1)} %copy-done, bf16[8,2,128,1024]{3,2,1,0:T(8,128)(2,1)S(1)} %copy-done.3), kind=kOutput, calls=%fused_computation.32 | convolution fusion | flops 1622409216 | bytes 16777216 | tf_op jit(solution)/shard_map/nlcd,ldf->nlcf/dot_general | solution.py:9
  267.3 1.1 copy-done.8
  268.4 6.3 %fusion.21 = f32[2,1024,384]{2,1,0:T(8,128)} fusion(bf16[8,2,128,384]{3,2,0,1:T(8,128)(2,1)S(1)} %get-tuple-element.28, f32[8,2,128]{2,0,1:T(8,128)S(1)} %copy_convert_fusion, bf16[8,2,128,1024]{3,2,1,0:T(8,128)(2,1)} %all-to-all-done.1), kind=kOutput, calls=%fused_computation.37 | convolution fusion | flops 1616904192 | bytes 8921088 | tf_op jit(solution)/shard_map/nlcd,nlcf->ldf/dot_general | solution.py:30
  274.7 0.0 reduce-scatter.8.cloned.1.call-update
  274.8 0.2 reduce-scatter.6.cloned.1.call-start
  275.0 6.7 %convolution_bitcast_fusion = f32[2,1024,384]{2,1,0:T(8,128)} fusion(bf16[8,2,128,1024]{3,2,1,0:T(8,128)(2,1)} %all_to_all.25, bf16[8,2,128,384]{3,2,0,1:T(8,128)(2,1)} %get-tuple-element.30), kind=kOutput, calls=%fused_computation.38 | convolution fusion | flops 1610612736 | bytes 8912896 | tf_op jit(solution)/shard_map/nlcd,nlcf->ldf/dot_general | solution.py:29
  281.7 0.0 reduce-scatter.6.cloned.1.call-update
  281.7 6.2 %fusion.1 = bf16[8,2,128]{2,0,1:T(8,128)(2,1)S(1)} fusion(bf16[8,2,128,1024]{3,2,1,0:T(8,128)(2,1)} %all-to-all-done.1, bf16[8,2,128,384]{3,2,0,1:T(8,128)(2,1)} %copy-done.8, bf16[2,1024,384]{2,1,0:T(8,128)(2,1)} %param.15), kind=kOutput, calls=%fused_computation.9 | convolution fusion | flops 1616902144 | bytes 7344128 | tf_op jit(solution)/shard_map/nlcf,ldf->nlcd/dot_general | solution.py:13
  287.9 0.6 copy.133
  288.5 3.9 all-to-all-start.4
  292.4 3.9 fusion.24
  296.3 2.4 fusion.2
  298.7 2.5 copy.132
  301.2 0.0 all-to-all-done.4
  301.2 6.1 %all-to-all-start.3 = ((bf16[8,2,128,1024]{3,2,1,0:T(8,128)(2,1)}), bf16[8,2,128,1024]{3,2,1,0:T(8,128)(2,1)}, u32[]{:S(2)}, u32[]{:S(2)}) async-start(bf16[8,2,128,1024]{3,2,1,0:T(8,128)(2,1)} %copy.132), calls=%async_computation.3 | async-start | bytes 8388608 | tf_op jit(solution)/shard_map/all_to_all | solution.py:79
  307.3 0.3 reduce-scatter.4.cloned.1.call-start
  307.6 6.3 %convolution_bitcast_fusion.1 = f32[2,1024,384]{2,1,0:T(8,128)} fusion(bf16[8,2,128,1024]{3,2,1,0:T(8,128)(2,1)} %all_to_all.25, bf16[8,2,128,384]{3,2,0,1:T(8,128)(2,1)S(1)} %copy-done.5), kind=kOutput, calls=%fused_computation.39 | convolution fusion | flops 1610612736 | bytes 8912896 | tf_op jit(solution)/shard_map/nlcd,nlcf->ldf/dot_general | solution.py:26
  313.9 0.0 reduce-scatter.4.cloned.1.call-update
  313.9 6.8 %gather_fusion.2 = bf16[1024]{0:T(1024)(128)(2,1)S(1)} fusion(bf16[2048]{0:T(1024)(128)(2,1)S(1)} %bitcast.89, s32[1024]{0:T(1024)S(1)} %broadcast_clamp_fusion.1), kind=kCustom, calls=%fused_computation.4 | custom fusion | bytes 8192 | tf_op jit(solution)/shard_map/jit(_take)/gather | solution.py:87
  320.7 0.1 gather.23
  320.8 0.1 copy.134
  320.9 0.6 broadcast_select_fusion.2
  321.5 0.1 copy.125
  321.6 0.0 reduce-scatter.8.cloned.1.call-done
  321.6 2.0 convert_element_type.56
  323.7 29.0 %reduce-scatter.6.cloned.1.call-done = f32[2,256,384]{2,1,0:T(8,128)} async-done(((f32[2,1024,384]{2,1,0:T(8,128)}), f32[2,256,384]{2,1,0:T(8,128)}) %reduce-scatter.6.cloned.1.call-update) | async-done | bytes 786448 | tf_op jit(solution)/shard_map/reduce_scatter | solution.py:93
  352.6 1.9 convert_element_type.55
  354.6 38.6 %reduce-scatter.4.cloned.1.call-done = f32[2,256,384]{2,1,0:T(8,128)} async-done(((f32[2,1024,384]{2,1,0:T(8,128)}), f32[2,256,384]{2,1,0:T(8,128)}) %reduce-scatter.4.cloned.1.call-update) | async-done | bytes 786448 | tf_op jit(solution)/shard_map/reduce_scatter | solution.py:92
  393.1 1.9 convert_element_type.54
  395.1 5.3 %all-to-all-done.3 = bf16[8,2,128,1024]{3,2,1,0:T(8,128)(2,1)} async-done(((bf16[8,2,128,1024]{3,2,1,0:T(8,128)(2,1)}), bf16[8,2,128,1024]{3,2,1,0:T(8,128)(2,1)}, u32[]{:S(2)}, u32[]{:S(2)}) %all-to-all-start.3) | async-done | bytes 4194336 | tf_op jit(solution)/shard_map/all_to_all | solution.py:79
  400.3 8.8 %gather_fusion.1 = bf16[1024,1024]{1,0:T(8,128)(2,1)} fusion(bf16[2048,1024]{1,0:T(8,128)(2,1)} %bitcast.15, s32[1024]{0:T(1024)S(1)} %broadcast_clamp_fusion.1), kind=kCustom, calls=%fused_computation.3 | custom fusion | bytes 4198400 | tf_op jit(solution)/shard_map/jit(_take)/gather | solution.py:82
  409.1 3.4 fusion.20
  (16 shorter events, 0.1 us)
Async XLA Ops:
  7.2 255.3 %copy-start = (bf16[2,1024,384]{2,1,0:T(8,128)(2,1)S(1)}, bf16[2,1024,384]{2,1,0:T(8,128)(2,1)}, u32[]{:S(2)}) copy-start(bf16[2,1024,384]{2,1,0:T(8,128)(2,1)} %param.14) | copy-start | bytes 4718596
  7.2 29.0 %copy-start.1 = (bf16[128,1024]{1,0:T(8,128)(2,1)S(1)}, bf16[128,1024]{1,0:T(8,128)(2,1)}, u32[]{:S(2)}) copy-start(bf16[128,1024]{1,0:T(8,128)(2,1)} %param.9) | copy-start | bytes 786436
  29.0 32.5 %all-to-all-start = ((bf16[8,2,128]{2,1,0:T(2,128)(2,1)}), bf16[8,2,128]{2,1,0:T(2,128)(2,1)S(1)}, u32[]{:S(2)}, u32[]{:S(2)}) async-start(bf16[8,2,128]{2,1,0:T(2,128)(2,1)} %bitcast.1), calls=%async_computation | async-start | bytes 8192 | tf_op jit(solution)/shard_map/all_to_all | solution.py:73
  36.2 9.7 %copy-start.2 = (bf16[128,1024]{1,0:T(8,128)(2,1)S(1)}, bf16[128,1024]{1,0:T(8,128)(2,1)}, u32[]{:S(2)}) copy-start(bf16[128,1024]{1,0:T(8,128)(2,1)} %param.10) | copy-start | bytes 786436
  160.4 4.8 %copy-start.4 = (bf16[2,1024,384]{2,1,0:T(8,128)(2,1)S(1)}, bf16[2,1024,384]{2,1,0:T(8,128)(2,1)}, u32[]{:S(2)}) copy-start(bf16[2,1024,384]{2,1,0:T(8,128)(2,1)} %param.13) | copy-start | bytes 4718596
  160.4 96.8 %all-to-all-start.1 = ((bf16[8,2,128,1024]{3,2,1,0:T(8,128)(2,1)}), bf16[8,2,128,1024]{3,2,1,0:T(8,128)(2,1)}, u32[]{:S(2)}, u32[]{:S(2)}) async-start(bf16[8,2,128,1024]{3,2,1,0:T(8,128)(2,1)} %bitcast.90), calls=%async_computation.1 | async-start | bytes 8388608 | tf_op jit(solution)/shard_map/all_to_all | solution.py:72
  165.1 156.5 %reduce-scatter.8.cloned.1.call-start = ((), (), s32[]{:S(2)}) async-start(), calls=%async_computation.10 | async-start | bytes 3932160 | tf_op jit(solution)/shard_map/reduce_scatter | solution.py:94
  257.2 5.2 %copy-start.3 = (bf16[8,2,128,1024]{3,2,1,0:T(8,128)(2,1)S(1)}, bf16[8,2,128,1024]{3,2,1,0:T(8,128)(2,1)}, u32[]{:S(2)}) copy-start(bf16[8,2,128,1024]{3,2,1,0:T(8,128)(2,1)} %all_to_all.25) | copy-start | bytes 12582916
  257.2 5.2 %copy-start.7 = (f32[2,8,128,384]{3,2,1,0:T(8,128)S(1)}, f32[2,8,128,384]{3,2,1,0:T(8,128)}, u32[]{:S(2)}) copy-start(f32[2,8,128,384]{3,2,1,0:T(8,128)} %fusion.3) | copy-start | bytes 9437188
  267.3 1.1 copy-start.8
  274.8 77.9 %reduce-scatter.6.cloned.1.call-start = ((), (), s32[]{:S(2)}) async-start(), calls=%async_computation.9 | async-start | bytes 3932160 | tf_op jit(solution)/shard_map/reduce_scatter | solution.py:93
  288.5 12.7 %all-to-all-start.4 = ((bf16[8,2,128]{2,1,0:T(2,128)(2,1)}), bf16[8,2,128]{2,1,0:T(2,128)(2,1)S(1)}, u32[]{:S(2)}, u32[]{:S(2)}) async-start(bf16[8,2,128]{2,1,0:T(2,128)(2,1)} %copy.133), calls=%async_computation.4 | async-start | bytes 8192 | tf_op jit(solution)/shard_map/all_to_all | solution.py:80
  292.4 3.9 copy-start.6
  301.2 6.4 %copy-start.5 = (bf16[8,2,128,384]{3,2,0,1:T(8,128)(2,1)S(1)}, bf16[8,2,128,384]{3,2,0,1:T(8,128)(2,1)}, u32[]{:S(2)}) copy-start(bf16[8,2,128,384]{3,2,0,1:T(8,128)(2,1)} %get-tuple-element.29) | copy-start | bytes 4718596
  301.2 99.1 %all-to-all-start.3 = ((bf16[8,2,128,1024]{3,2,1,0:T(8,128)(2,1)}), bf16[8,2,128,1024]{3,2,1,0:T(8,128)(2,1)}, u32[]{:S(2)}, u32[]{:S(2)}) async-start(bf16[8,2,128,1024]{3,2,1,0:T(8,128)(2,1)} %copy.132), calls=%async_computation.3 | async-start | bytes 8388608 | tf_op jit(solution)/shard_map/all_to_all | solution.py:79
  307.3 85.8 %reduce-scatter.4.cloned.1.call-start = ((), (), s32[]{:S(2)}) async-start(), calls=%async_computation.8 | async-start | bytes 3932160 | tf_op jit(solution)/shard_map/reduce_scatter | solution.py:92
Sparse Core Ops, SparseCore 0:
  274.9 37.0 reduce-scatter.7
  314.7 37.9 reduce-scatter.5
  355.2 37.9 reduce-scatter.3
where the time goes:
time: 420 us; the launch traced here: 419 us
  waiting for transfers between devices  159 us (38%)
  blocking collectives  98.9 us (24%)
  local copies, waits for them, and re-layouts  58.2 us (14%)
  matrix products  47.9 us (11%)
  starting transfers between devices  22.5 us (5%)
  other arithmetic  18.8 us (4%)
  between operations  14 us (3%)
    all_to_all x1, blocking collectives, body(): lax.all_to_all(send_x, 'expert', split_axis=0, concat_axis=0, tiled=True)  98.9 us
    all_to_all x1, waiting for transfers between devices, body(): lax.all_to_all(send_g, 'expert', split_axis=0, concat_axis=0, tiled=True)  85.9 us
    reduce_scatter x1, waiting for transfers between devices, body(): lax.psum_scatter(grad_gate_w, 'dp', scatter_dimension=1, tiled=True)  38.6 us
    reduce_scatter x1, waiting for transfers between devices, body(): lax.psum_scatter(grad_up_w, 'dp', scatter_dimension=1, tiled=True)  29 us
    gather x1, local copies, waits for them, and re-layouts, body(): jnp.take(route_weight.reshape(-1), slot_route, axis=0, mode='fill', fill_...  13.1 us
    gather x1, local copies, waits for them, and re-layouts, body(): jnp.take(cotangent, slot_token, axis=0, mode='fill', fill_value=0)  9.69 us
    gather x1, local copies, waits for them, and re-layouts, body(): jnp.take(tokens, slot_token, axis=0, mode='fill', fill_value=0)  9.66 us
    gather x1, local copies, waits for them, and re-layouts, body(): jnp.take(back_rows.reshape(slot_total, model_width), slot_index, axis=0,...  8.75 us
  transfers between devices with their start and end apart: 7, of which 4 were waited for; matrix products, arithmetic and copies ran while one was open for 18% of the time, Pallas kernels for 0%

commit v1 on v0

v1 whole, which is shorter than its diff:
```python
import jax
import jax.numpy as jnp
from jax import lax
from jax.sharding import PartitionSpec as P


def dot(a, b, dims):
    return lax.dot_general(a, b, (dims, ((), ())), preferred_element_type=jnp.float32)


def body(tokens, cotangent, routes, route_weight, w_gate, w_up, w_down):
    local = w_gate.shape[0]
    groups = lax.axis_size("expert")
    experts = local * groups
    rows = tokens.shape[0]
    ids = jnp.arange(experts, dtype=jnp.int32)
    chosen = routes[:, :, None] == ids[None, None, :]
    dense = jnp.sum(jnp.where(chosen, route_weight.astype(jnp.float32)[:, :, None], 0.0), axis=1)
    dense = dense.astype(jnp.bfloat16)
    x = lax.all_gather(tokens, "expert", tiled=True)
    g = lax.all_gather(cotangent, "expert", tiled=True)
    wt = lax.all_to_all(
        dense.reshape(rows, groups, local).transpose(1, 0, 2), "expert", 0, 0, tiled=True
    ).reshape(groups * rows, local)
    grad_rows = 0.0
    scores = []
    gg, gu, gd = [], [], []
    for l in range(local):
        w = wt[:, l : l + 1].astype(jnp.float32)
        a = dot(x, w_gate[l], ((1,), (0,)))
        u = dot(x, w_up[l], ((1,), (0,)))
        q = dot(g, w_down[l], ((1,), (0,)))
        s = jax.nn.sigmoid(a)
        silu = a * s
        h = silu * u
        scores.append(jnp.sum(h * q, axis=1))
        hw = (h * w).astype(jnp.bfloat16)
        wq = w * q
        dg = (wq * u * (s * (1.0 + a * (1.0 - s)))).astype(jnp.bfloat16)
        du = (wq * silu).astype(jnp.bfloat16)
        grad_rows = grad_rows + dot(dg, w_gate[l], ((1,), (1,))) + dot(du, w_up[l], ((1,), (1,)))
        gg.append(dot(x, dg, ((0,), (0,))))
        gu.append(dot(x, du, ((0,), (0,))))
        gd.append(dot(g, hw, ((0,), (0,))))
    grad_tokens = lax.psum_scatter(
        grad_rows.astype(jnp.bfloat16), "expert", scatter_dimension=0, tiled=True
    )
    score = jnp.stack(scores, axis=1).astype(jnp.bfloat16)
    back = lax.all_to_all(score.reshape(groups, rows, local), "expert", 0, 0, tiled=True)
    back = back.transpose(1, 0, 2).reshape(rows, experts).astype(jnp.float32)
    grw = jnp.sum(jnp.where(chosen, back[:, None, :], 0.0), axis=2)

    def over_dp(parts):
        return lax.psum_scatter(
            jnp.stack(parts).astype(jnp.bfloat16), "dp", scatter_dimension=1, tiled=True
        )

    return (
        grad_tokens.astype(jnp.bfloat16),
        grw.astype(jnp.bfloat16),
        over_dp(gg),
        over_dp(gu),
        over_dp(gd),
    )


def solution(mesh):
    return jax.shard_map(
        body,
        mesh=mesh,
        in_specs=(P(("dp", "expert"), None),) * 4 + (P("expert", None, None),) * 3,
        out_specs=(P(("dp", "expert"), None),) * 2 + (P("expert", "dp", None),) * 3,
        check_vma=False,
    )
```

time: 420 us -> 311 us (0.74)
  blocking collectives: 98.9 us -> 8.82 us
  waiting for transfers between devices: 159 us -> 232 us
  local copies, waits for them, and re-layouts: 58.2 us -> 9.55 us
  starting transfers between devices: 22.5 us -> 3.74 us
  matrix products: 47.9 us -> 33.5 us
  other arithmetic: 18.8 us -> 8.73 us
    all_gather x0 -> x2, waiting for transfers between devices: none -> 94.7 us  [the longest x1 53.5 us: body(): x = lax.all_gather(tokens, 'expert', tiled=True)]
    all_to_all x1, blocking collectives: 98.9 us -> 8.82 us  [body(): lax.all_to_all(dense.reshape(rows, groups, local).transpose(1, 0, 2), 'ex...]
    all_to_all x4 -> x1, waiting for transfers between devices: 91.1 us -> 6.25 us  [body(): lax.all_to_all(score.reshape(groups, rows, local), 'expert', 0, 0, tiled=...]
    reduce_scatter x3 -> x4, waiting for transfers between devices: 67.6 us -> 130 us  [the longest x1 70.3 us: body(): lax.psum_scatter(grad_rows.astype(jnp.bfloat16), 'expert', scatter_dimens...]
    gather x7 -> x0, local copies, waits for them, and re-layouts: 48.1 us -> none  [the longest x1 13.1 us: body(): jnp.take(route_weight.reshape(-1), slot_route, axis=0, mode='fill', fill_...]
    all_to_all x4 -> x1, starting transfers between devices: 21.9 us -> 3.31 us  [body(): lax.all_to_all(score.reshape(groups, rows, local), 'expert', 0, 0, tiled=...]
    dot_general x9 -> x16, matrix products: 47.9 us -> 33.5 us  [dot(): lax.dot_general(a, b, (dims, ((), ())), preferred_element_type=jnp.float32)]
    select_n x5 -> x0, other arithmetic: 7.77 us -> none  [the longest x1 5.85 us: body(): jnp.take(cotangent, slot_token, axis=0, mode='fill', fill_value=0)]
  transfers between devices with their start and end apart: 7 -> 7, of which waited for: 4 -> 7; matrix products, arithmetic and copies ran while one was open for 18% -> 11% of each run, Pallas kernels for 0% -> 0%
where the time goes in v1:
time: 311 us
  waiting for transfers between devices  232 us (75%)
  matrix products  33.5 us (11%)
  between operations  14.4 us (5%)
  local copies, waits for them, and re-layouts  9.55 us (3%)
  blocking collectives  8.82 us (3%)
  other arithmetic  8.73 us (3%)
  starting transfers between devices  3.74 us (1%)
    reduce_scatter x1, waiting for transfers between devices, body(): lax.psum_scatter(grad_rows.astype(jnp.bfloat16), 'expert', scatter_dimens...  70.3 us
    reduce_scatter x3, waiting for transfers between devices, over_dp(): lax.psum_scatter(jnp.stack(parts).astype(jnp.bfloat16), 'dp', scatter_dim...  59.4 us
    all_gather x1, waiting for transfers between devices, body(): x = lax.all_gather(tokens, 'expert', tiled=True)  53.5 us
    all_gather x1, waiting for transfers between devices, body(): g = lax.all_gather(cotangent, 'expert', tiled=True)  41.2 us
    dot_general x16, matrix products, dot(): lax.dot_general(a, b, (dims, ((), ())), preferred_element_type=jnp.float32)  33.5 us
    unnamed x43, local copies, waits for them, and re-layouts  8.96 us
    all_to_all x1, blocking collectives, body(): lax.all_to_all(dense.reshape(rows, groups, local).transpose(1, 0, 2), 'ex...  8.82 us
    all_to_all x1, waiting for transfers between devices, body(): lax.all_to_all(score.reshape(groups, rows, local), 'expert', 0, 0, tiled=...  6.25 us
  transfers between devices with their start and end apart: 7, of which 7 were waited for; matrix products, arithmetic and copies ran while one was open for 11% of the time, Pallas kernels for 0%

profile of v1, /device:TPU:0, one launch (start us, length us, event | category | flops | bytes accessed | tf_op | source)
XLA Modules:
  0.0 310.8 jit_solution(1147049736414003773)
XLA Ops:
  7.2 0.0 all-gather.5.cloned.1.call-start
  7.2 0.7 all-gather.5.cloned.1.call-update
  7.9 0.0 all-gather.3.cloned.1.call-start
  7.9 0.7 all-gather.3.cloned.1.call-update
  8.6 0.0 copy-start.2
  8.7 53.5 %all-gather.5.cloned.1.call-done = bf16[1024,1024]{1,0:T(8,128)(2,1)} async-done(((bf16[128,1024]{1,0:T(8,128)(2,1)}), bf16[1024,1024]{1,0:T(8,128)(2,1)}) %all-gather.5.cloned.1.call-update) | async-done | bytes 2097168 | tf_op jit(solution)/shard_map/all_gather | solution.py:20
  62.1 4.1 %fusion.10 = f32[1024,384]{0,1:T(8,128)} fusion(bf16[1024,1024]{1,0:T(8,128)(2,1)} %all-gather.5.cloned.1.call-done, bf16[2,1024,384]{2,1,0:T(8,128)(2,1)} %param.11), kind=kOutput, calls=%fused_computation.30 | convolution fusion | flops 805306368 | bytes 4456448 | tf_op jit(solution)/shard_map/dot_general | solution.py:8
  66.2 0.0 copy-done.2
  66.2 1.1 fusion.19
  67.3 0.3 copy-done
  67.6 2.2 fusion.13
  69.8 1.0 fusion.23
  70.9 0.0 copy-start.6
  70.9 41.2 %all-gather.3.cloned.1.call-done = bf16[1024,1024]{1,0:T(8,128)(2,1)} async-done(((bf16[128,1024]{1,0:T(8,128)(2,1)}), bf16[1024,1024]{1,0:T(8,128)(2,1)}) %all-gather.3.cloned.1.call-update) | async-done | bytes 2097168 | tf_op jit(solution)/shard_map/all_gather | solution.py:21
  112.1 4.3 %multiply_reduce_fusion.1 = (bf16[1024]{0:T(1024)(128)(2,1)S(1)}, f32[1024,384]{0,1:T(8,128)}) fusion(f32[1024,384]{0,1:T(8,128)S(1)} %fusion.23, f32[1024,384]{0,1:T(8,128)S(1)} %fusion.19, bf16[1024,1024]{1,0:T(8,128)(2,1)} %all-gather.3.cloned.1.call-done, bf16[2,1024,384]{2,1,0:T(8,128)(2,1)} %param.13), kind=kOutput, calls=%fused_computation.7 | convolution fusion | flops 808057856 | bytes 7604224 | tf_op jit(solution)/shard_map/dot_general | solution.py:8
  116.4 0.0 copy-done.17
  116.4 0.0 copy-start.13
  116.4 0.0 copy-start.12
  116.4 2.5 multiply_reduce_fusion
  118.9 0.6 copy.31
  119.5 3.3 %all-to-all-start.1 = ((bf16[8,128,2]{1,2,0:T(2,128)(2,1)}), bf16[8,128,2]{1,2,0:T(2,128)(2,1)S(1)}, u32[]{:S(2)}, u32[]{:S(2)}) async-start(bf16[8,128,2]{1,2,0:T(2,128)(2,1)} %copy.31), calls=%async_computation.2 | async-start | bytes 8192 | tf_op jit(solution)/shard_map/all_to_all | solution.py:49
  122.8 0.0 reduce-scatter.11.cloned.1.call-start
  122.9 6.3 %all-to-all-done.1 = bf16[8,128,2]{1,2,0:T(2,128)(2,1)S(1)} async-done(((bf16[8,128,2]{1,2,0:T(2,128)(2,1)}), bf16[8,128,2]{1,2,0:T(2,128)(2,1)S(1)}, u32[]{:S(2)}, u32[]{:S(2)}) %all-to-all-start.1) | async-done | bytes 4128 | tf_op jit(solution)/shard_map/all_to_all | solution.py:49
  129.2 0.0 copy-done.12
  129.2 0.6 select_reduce_fusion
  129.8 8.8 %all_to_all.10 = bf16[8,128,2]{1,2,0:T(2,128)(2,1)S(1)} all-to-all(bf16[8,128,2]{1,2,0:T(2,128)(2,1)S(1)} %bitcast.91), channel_id=1, replica_groups=mesh['dp'=4,'expert'=8] {'expert'}, dimensions={0} | all-to-all | bytes 8192 | tf_op jit(solution)/shard_map/all_to_all | solution.py:22
  138.6 0.0 copy-start.18
  138.6 3.7 %fusion.7 = bf16[1,1024,384]{1,2,0:T(8,128)(2,1)S(1)} fusion(bf16[1024,1024]{1,0:T(8,128)(2,1)} %all-gather.3.cloned.1.call-done, f32[1024]{0:T(1024)S(1)} %bitcast.94, f32[1024,384]{0,1:T(8,128)} %fusion.13, f32[1024,384]{0,1:T(8,128)} %fusion.10), kind=kOutput, calls=%fused_computation.27 | convolution fusion | flops 808452096 | bytes 6033408 | tf_op jit(solution)/shard_map/dot_general | solution.py:8
  142.4 1.1 fusion.6
  143.5 1.3 pad_maximum_fusion.2
  144.8 0.0 reduce-scatter.11.cloned.1.call-update
  144.8 0.2 reduce-scatter.9.cloned.1.call-start
  145.0 1.2 copy-done.10
  146.2 3.2 %multiply_convert_fusion.2 = (bf16[1024,384]{0,1:T(8,128)(2,1)S(1)}, bf16[1024,384]{0,1:T(8,128)(2,1)S(1)}) fusion(f32[1024,384]{0,1:T(8,128)} %get-tuple-element.34, f32[1024]{0:T(1024)S(1)} %bitcast.95, f32[1024,384]{0,1:T(8,128)S(1)} %copy-done.10, f32[1024,384]{0,1:T(8,128)} %fusion.13), kind=kLoop, calls=%fused_computation.8 | loop fusion | flops 5505024 | bytes 6295552 | tf_op jit(solution)/shard_map/convert_element_type | solution.py:40
  149.5 1.0 fusion.5
  150.5 0.5 copy-done.5
  151.0 0.5 copy-done.7
  151.5 0.5 copy-done.8
  152.0 1.0 multiply_convert_fusion.4
  153.0 1.0 fusion.4
  154.0 1.3 pad_maximum_fusion.1
  155.3 0.0 reduce-scatter.9.cloned.1.call-update
  155.3 0.0 reduce-scatter.7.cloned.1.call-start
  155.4 2.7 fusion.3
  158.1 0.0 copy-done.16
  158.1 1.0 fusion.2
  159.1 1.3 pad_maximum_fusion
  160.4 0.0 reduce-scatter.7.cloned.1.call-update
  160.5 0.0 reduce-scatter.5.cloned.1.call-start
  160.5 0.0 copy-start.1
  160.5 2.6 fusion.17
  163.1 0.0 copy-start.3
  163.1 1.3 fusion.21
  164.4 0.1 copy-done.3
  164.5 1.3 fusion.8
  165.8 2.7 add_convert_fusion
  168.5 0.0 reduce-scatter.5.cloned.1.call-update
  168.6 1.8 reduce-scatter.11.cloned.1.call-done
  170.4 1.9 copy.34
  172.3 28.8 %reduce-scatter.9.cloned.1.call-done = bf16[2,256,384]{1,2,0:T(8,128)(2,1)} async-done(((bf16[2,1024,384]{1,2,0:T(8,128)(2,1)}), bf16[2,256,384]{1,2,0:T(8,128)(2,1)}) %reduce-scatter.9.cloned.1.call-update) | async-done | bytes 393232 | tf_op jit(solution)/shard_map/reduce_scatter | solution.py:54
  201.1 1.9 copy.33
  203.1 28.7 %reduce-scatter.7.cloned.1.call-done = bf16[2,256,384]{1,2,0:T(8,128)(2,1)} async-done(((bf16[2,1024,384]{1,2,0:T(8,128)(2,1)}), bf16[2,256,384]{1,2,0:T(8,128)(2,1)}) %reduce-scatter.7.cloned.1.call-update) | async-done | bytes 393232 | tf_op jit(solution)/shard_map/reduce_scatter | solution.py:54
  231.7 1.9 copy.32
  233.7 70.3 %reduce-scatter.5.cloned.1.call-done = bf16[128,1024]{1,0:T(8,128)(2,1)} async-done(((bf16[1024,1024]{1,0:T(8,128)(2,1)}), bf16[128,1024]{1,0:T(8,128)(2,1)}) %reduce-scatter.5.cloned.1.call-update) | async-done | bytes 262160 | tf_op jit(solution)/shard_map/reduce_scatter | solution.py:45
  (27 shorter events, 0.1 us)
Async XLA Ops:
  7.2 55.0 %all-gather.5.cloned.1.call-start = ((), (), s32[]{:S(2)}) async-start(), calls=%async_computation.7 | async-start | bytes 2359296 | tf_op jit(solution)/shard_map/all_gather | solution.py:20
  7.9 104.2 %all-gather.3.cloned.1.call-start = ((), (), s32[]{:S(2)}) async-start(), calls=%async_computation.6 | async-start | bytes 2359296 | tf_op jit(solution)/shard_map/all_gather | solution.py:21
  8.6 57.6 %copy-start.2 = (bf16[2,1024,384]{2,1,0:T(8,128)(2,1)S(1)}, bf16[2,1024,384]{2,1,0:T(8,128)(2,1)}, u32[]{:S(2)}) copy-start(bf16[2,1024,384]{2,1,0:T(8,128)(2,1)} %param.11) | copy-start | bytes 4718596
  62.1 4.1 %copy-start.14 = (bf16[1024,1024]{1,0:T(8,128)(2,1)S(1)}, bf16[1024,1024]{1,0:T(8,128)(2,1)}, u32[]{:S(2)}) copy-start(bf16[1024,1024]{1,0:T(8,128)(2,1)} %all-gather.5.cloned.1.call-done) | copy-start | bytes 6291460
  66.2 1.4 copy-start
  67.6 74.7 %copy-start.4 = (f32[1024,384]{0,1:T(8,128)}, f32[1024,384]{0,1:T(8,128)S(1)}, u32[]{:S(2)}) copy-start(f32[1024,384]{0,1:T(8,128)S(1)} %fusion.19) | copy-start | bytes 4718596
  70.9 71.5 %copy-start.6 = (f32[1024,384]{0,1:T(8,128)}, f32[1024,384]{0,1:T(8,128)S(1)}, u32[]{:S(2)}) copy-start(f32[1024,384]{0,1:T(8,128)S(1)} %fusion.23) | copy-start | bytes 4718596
  112.1 4.3 %copy-start.9 = (f32[1024,384]{0,1:T(8,128)S(1)}, f32[1024,384]{0,1:T(8,128)}, u32[]{:S(2)}) copy-start(f32[1024,384]{0,1:T(8,128)} %fusion.10) | copy-start | bytes 4718596
  112.1 4.3 %copy-start.11 = (f32[1024,384]{0,1:T(8,128)S(1)}, f32[1024,384]{0,1:T(8,128)}, u32[]{:S(2)}) copy-start(f32[1024,384]{0,1:T(8,128)} %fusion.13) | copy-start | bytes 4718596
  112.1 4.3 %copy-start.17 = (bf16[1024,1024]{1,0:T(8,128)(2,1)S(1)}, bf16[1024,1024]{1,0:T(8,128)(2,1)}, u32[]{:S(2)}) copy-start(bf16[1024,1024]{1,0:T(8,128)(2,1)} %all-gather.3.cloned.1.call-done) | copy-start | bytes 6291460
  112.1 4.3 %copy-start.19 = (bf16[2,1024,384]{2,1,0:T(8,128)(2,1)S(1)}, bf16[2,1024,384]{2,1,0:T(8,128)(2,1)}, u32[]{:S(2)}) copy-start(bf16[2,1024,384]{2,1,0:T(8,128)(2,1)} %param.13) | copy-start | bytes 4718596
  116.4 6.5 %copy-start.13 = (bf16[128,8]{0,1:T(8,128)(2,1)S(1)}, bf16[128,8]{0,1:T(8,128)(2,1)}, u32[]{:S(2)}) copy-start(bf16[128,8]{0,1:T(8,128)(2,1)} %param.10) | copy-start | bytes 6148
  116.4 12.8 %copy-start.12 = (s32[128,8]{0,1:T(8,128)S(1)}, s32[128,8]{0,1:T(8,128)}, u32[]{:S(2)}) copy-start(s32[128,8]{0,1:T(8,128)} %param.9) | copy-start | bytes 12292
  119.5 9.6 %all-to-all-start.1 = ((bf16[8,128,2]{1,2,0:T(2,128)(2,1)}), bf16[8,128,2]{1,2,0:T(2,128)(2,1)S(1)}, u32[]{:S(2)}, u32[]{:S(2)}) async-start(bf16[8,128,2]{1,2,0:T(2,128)(2,1)} %copy.31), calls=%async_computation.2 | async-start | bytes 8192 | tf_op jit(solution)/shard_map/all_to_all | solution.py:49
  122.8 47.6 %reduce-scatter.11.cloned.1.call-start = ((), (), s32[]{:S(2)}) async-start(), calls=%async_computation.11 | async-start | bytes 1966080 | tf_op jit(solution)/shard_map/reduce_scatter | solution.py:54
  138.6 3.8 %copy-start.18 = (bf16[1024,1024]{1,0:T(8,128)(2,1)S(1)}, bf16[1024,1024]{1,0:T(8,128)(2,1)}, u32[]{:S(2)}) copy-start(bf16[1024,1024]{1,0:T(8,128)(2,1)} %all-gather.3.cloned.1.call-done) | copy-start | bytes 6291460
  144.8 1.4 copy-start.10
  144.8 56.3 %reduce-scatter.9.cloned.1.call-start = ((), (), s32[]{:S(2)}) async-start(), calls=%async_computation.10 | async-start | bytes 1966080 | tf_op jit(solution)/shard_map/reduce_scatter | solution.py:54
  146.2 3.2 %copy-start.15 = (bf16[1024,1024]{1,0:T(8,128)(2,1)S(1)}, bf16[1024,1024]{1,0:T(8,128)(2,1)}, u32[]{:S(2)}) copy-start(bf16[1024,1024]{1,0:T(8,128)(2,1)} %all-gather.5.cloned.1.call-done) | copy-start | bytes 6291460
  149.4 1.5 copy-start.5
  149.4 2.1 copy-start.7
  149.5 2.6 copy-start.8
  155.3 76.4 %reduce-scatter.7.cloned.1.call-start = ((), (), s32[]{:S(2)}) async-start(), calls=%async_computation.9 | async-start | bytes 1966080 | tf_op jit(solution)/shard_map/reduce_scatter | solution.py:54
  155.4 2.7 copy-start.16
  160.5 143.5 %reduce-scatter.5.cloned.1.call-start = ((), (), s32[]{:S(2)}) async-start(), calls=%async_computation.8 | async-start | bytes 2359296 | tf_op jit(solution)/shard_map/reduce_scatter | solution.py:45
  160.5 2.6 copy-start.1
  163.1 1.4 copy-start.3
Sparse Core Ops, SparseCore 0:
  10.1 51.9 all-gather.4
  64.3 47.7 all-gather.2
  144.9 25.4 reduce-scatter.10
  172.9 28.1 reduce-scatter.8
  203.5 28.1 reduce-scatter.6
  236.1 67.7 reduce-scatter.4

commit v2 on v1

--- a/solution.py
+++ b/solution.py
@@ -1,6 +1,10 @@
+import functools
+
 import jax
 import jax.numpy as jnp
 from jax import lax
+from jax.experimental import pallas as pl
+from jax.experimental.pallas import tpu as pltpu
 from jax.sharding import PartitionSpec as P
 
 
@@ -64,9 +68,424 @@
     )
 
 
+F32 = jnp.float32
+BF16 = jnp.bfloat16
+UP, DOWN, ACROSS = 0, 1, 2
+
+
+def visit(z, step, depth):
+    mirrored = 2 * z >= depth
+    base = jnp.where(mirrored, depth - 1 - z, z)
+    half = (step + 1) // 2
+    near = jnp.where(step % 2 == 1, base - half, base + half)
+    order = jnp.where(step <= 2 * base, near, step)
+    return jnp.where(mirrored, depth - 1 - order, order)
+
+
+def kernel(
+    depth,
+    tokens,
+    cotangent,
+    routes,
+    route_weight,
+    w_gate,
+    w_up,
+    w_down,
+    out_tokens,
+    out_weight,
+    out_gate,
+    out_up,
+    out_down,
+    xg,
+    gg,
+    wg,
+    wu,
+    wd,
+    dg,
+    du,
+    hw,
+    part,
+    part_in,
+    red,
+    red_in,
+    core_out,
+    core_in,
+    y_out,
+    y_in,
+    acc,
+    load_sem,
+    send_x,
+    send_g,
+    recv_x,
+    recv_g,
+    send_p,
+    recv_p,
+    send_r,
+    recv_r,
+    send_c,
+    recv_c,
+    send_y,
+    recv_y,
+):
+    rows, width = tokens.shape
+    local, _, ff = w_gate.shape
+    top = routes.shape[1]
+    wide = local * ff
+    full = width + 128
+    slab = out_gate.shape[1]
+    e = lax.axis_index("expert")
+    dp = lax.axis_index("dp")
+    z, x = e // 2, e % 2
+    y, core = dp // 2, dp % 2
+    partner = z * 2 + 1 - x
+    core_peer = y * 2 + 1 - core
+    y_peer = (1 - y) * 2 + core
+
+    loads = []
+    for i, (source, target) in enumerate(((w_gate, wg), (w_up, wu), (w_down, wd))):
+        for l in range(local):
+            loads.append(
+                pltpu.make_async_copy(
+                    source.at[l], target.at[:, pl.ds(l * ff, ff)], load_sem.at[i * local + l]
+                )
+            )
+    for c in loads:
+        c.start()
+
+    barrier = pltpu.get_barrier_semaphore()
+    pl.semaphore_signal(barrier, 1, device_id={"expert": partner}, device_id_type=pl.DeviceIdType.MESH)
+    for k in range(1, depth):
+        other = ((z + k) % depth) * 2 + x
+        pl.semaphore_signal(barrier, 1, device_id={"expert": other}, device_id_type=pl.DeviceIdType.MESH)
+    pl.semaphore_signal(barrier, 1, device_id={"dp": core_peer}, device_id_type=pl.DeviceIdType.MESH)
+    pl.semaphore_signal(barrier, 1, device_id={"dp": y_peer}, device_id_type=pl.DeviceIdType.MESH)
+
+    def block(i, n=rows):
+        return pl.ds(pl.multiple_of(i * n, n), n)
+
+    lane = lax.broadcasted_iota(jnp.int32, (rows, 128), 1)
+    dense = jnp.zeros((rows, 128), F32)
+    weights = route_weight[...].astype(F32)
+    for k in range(top):
+        dense = dense + jnp.where(routes[:, k : k + 1] == lane, weights[:, k : k + 1], 0.0)
+    xg[block(e), pl.ds(0, width)] = tokens[...]
+    xg[block(e), pl.ds(width, 128)] = dense.astype(BF16)
+    gg[block(e), :] = cotangent[...]
+    pl.semaphore_wait(barrier, depth + 2)
+
+    def move(buf, send, recv, i, way, target):
+        return pltpu.make_async_remote_copy(
+            buf.at[block(i)],
+            buf.at[block(i)],
+            send.at[i * 3 + way],
+            recv.at[i],
+            device_id={"expert": target},
+            device_id_type=pl.DeviceIdType.MESH,
+        )
+
+    pairs = ((xg, send_x, recv_x), (gg, send_g, recv_g))
+
+    def up(p, i):
+        return move(*p, i, UP, e + 2)
+
+    def down(p, i):
+        return move(*p, i, DOWN, e - 2)
+
+    def across(p, i):
+        return move(*p, i, ACROSS, partner)
+
+    for p in pairs:
+
+        @pl.when(z < depth - 1)
+        def _():
+            up(p, e).start()
+
+        @pl.when(z > 0)
+        def _():
+            down(p, e).start()
+
+        across(p, e).start()
+    for c in loads:
+        c.wait()
+
+    column = lax.broadcasted_iota(jnp.int32, (128, wide), 1)
+    owner = lax.broadcasted_iota(jnp.int32, (128, wide), 0) - e * local
+    hit = jnp.zeros((128, wide), F32)
+    for l in range(local):
+        inside = (column >= l * ff) & (column < (l + 1) * ff) & (owner == l)
+        hit = hit + jnp.where(inside, 1.0, 0.0)
+    hit = hit.astype(BF16)
+
+    def share(zz):
+        return pltpu.make_async_remote_copy(
+            part.at[block(zz * 2 + 1 - x)],
+            part_in.at[block(zz)],
+            send_p.at[zz],
+            recv_p.at[zz],
+            device_id={"expert": partner},
+            device_id_type=pl.DeviceIdType.MESH,
+        )
+
+    def home(zz):
+        return pltpu.make_async_remote_copy(
+            red.at[block(zz)],
+            red_in.at[block(z)],
+            send_r.at[zz],
+            recv_r.at[z],
+            device_id={"expert": zz * 2 + x},
+            device_id_type=pl.DeviceIdType.MESH,
+        )
+
+    def landed(zz):
+        return pltpu.make_async_remote_copy(
+            red.at[block(zz)],
+            red_in.at[block(zz)],
+            send_r.at[zz],
+            recv_r.at[zz],
+            device_id={"expert": zz * 2 + x},
+            device_id_type=pl.DeviceIdType.MESH,
+        )
+
+    def reduce(zz):
+        share(zz).wait_recv()
+        total = part[block(zz * 2 + x), :].astype(F32) + part_in[block(zz), :].astype(F32)
+        red[block(zz), :] = total.astype(BF16)
+
+        @pl.when(zz != z)
+        def _():
+            home(zz).start()
+
+    def work(zz):
+        here = block(zz, 2 * rows)
+        xs = xg[here, pl.ds(0, width)]
+        ws = xg[here, pl.ds(width, 128)]
+        gs = gg[here, :]
+        score = jnp.zeros((2 * rows, 128), F32)
+        cut = 256
+        for f in range(0, wide, cut):
+            cols = pl.ds(f, cut)
+            pick = hit[:, f : f + cut]
+            w = dot(ws, pick, ((1,), (0,)))
+            a = dot(xs, wg[:, cols], ((1,), (0,)))
+            u = dot(xs, wu[:, cols], ((1,), (0,)))
+            q = dot(gs, wd[:, cols], ((1,), (0,)))
+            s = 1.0 / (1.0 + jnp.exp(-a))
+            silu = a * s
+            h = silu * u
+            score = score + dot((h * q).astype(BF16), pick, ((1,), (1,)))
+            wq = w * q
+            hw[here, cols] = (h * w).astype(BF16)
+            dg[here, cols] = (wq * u * (s * (1.0 + a * (1.0 - s)))).astype(BF16)
+            du[here, cols] = (wq * silu).astype(BF16)
+        part[here, pl.ds(width, 128)] = score.astype(BF16)
+        for d in range(0, width, 256):
+            cols = pl.ds(d, 256)
+            back = dot(dg[here, :], wg[cols, :], ((1,), (1,)))
+            back = back + dot(du[here, :], wu[cols, :], ((1,), (1,)))
+            part[here, cols] = back.astype(BF16)
+
+    def step(s, carry):
+        d = s + 1
+
+        @pl.when(z - d >= 0)
+        def _():
+            i = e - 2 * d
+            for p in pairs:
+                up(p, i).wait_recv()
+
+                @pl.when(z < depth - 1)
+                def _():
+                    up(p, i).start()
+
+                across(p, i).start()
+
+        @pl.when(z + d < depth)
+        def _():
+            i = e + 2 * d
+            for p in pairs:
+                down(p, i).wait_recv()
+
+                @pl.when(z > 0)
+                def _():
+                    down(p, i).start()
+
+                across(p, i).start()
+
+        zz = visit(z, s, depth)
+        for p in pairs:
+            across(p, zz * 2 + 1 - x).wait_recv()
+        work(zz)
+        share(zz).start()
+
+        @pl.when(s > 0)
+        def _():
+            reduce(visit(z, s - 1, depth))
+
+        return carry
+
+    lax.fori_loop(0, depth, step, 0)
+
+    def slab_grads(c):
+        cols = pl.ds(pl.multiple_of(c * slab, slab), slab)
+        xt = xg[:, cols].T
+        yield dot(xt, dg[...], ((1,), (0,)))
+        yield dot(xt, du[...], ((1,), (0,)))
+        yield dot(gg[:, cols].T, hw[...], ((1,), (0,)))
+
+    def to_core(half, i):
+        k = half * 3 + i
+        return pltpu.make_async_remote_copy(
+            core_out.at[k],
+            core_in.at[k],
+            send_c.at[k],
+            recv_c.at[k],
+            device_id={"dp": core_peer},
+            device_id_type=pl.DeviceIdType.MESH,
+        )
+
+    def to_y(i):
+        return pltpu.make_async_remote_copy(
+            y_out.at[i],
+            y_in.at[i],
+            send_y.at[i],
+            recv_y.at[i],
+            device_id={"dp": y_peer},
+            device_id_type=pl.DeviceIdType.MESH,
+        )
+
+    for i, g in enumerate(slab_grads((1 - y) * 2 + 1 - core)):
+        core_out[i] = g.astype(BF16)
+        to_core(0, i).start()
+    reduce(visit(z, depth - 1, depth))
+    for i, g in enumerate(slab_grads(y_peer)):
+        acc[i] = g
+        to_core(0, i).wait_recv()
+        y_out[i] = (acc[i] + core_in[i].astype(F32)).astype(BF16)
+        to_y(i).start()
+    for i, g in enumerate(slab_grads(core_peer)):
+        core_out[3 + i] = g.astype(BF16)
+        to_core(1, i).start()
+    for i, g in enumerate(slab_grads(dp)):
+        acc[i] = g
+
+    total = red[block(z), :].astype(F32)
+    for k in range(1, depth):
+        zz = (z + k) % depth
+        landed(zz).wait_recv()
+        total = total + red_in[block(zz), :].astype(F32)
+    out_tokens[...] = total[:, :width].astype(BF16)
+    scores = total[:, width:full]
+    for k in range(top):
+        mine = jnp.where(routes[:, k : k + 1] == lane, scores, 0.0)
+        out_weight[:, k : k + 1] = jnp.sum(mine, axis=1, keepdims=True).astype(BF16)
+
+    for i, out in enumerate((out_gate, out_up, out_down)):
+        to_core(1, i).wait_recv()
+        to_y(i).wait_recv()
+        g = acc[i] + core_in[3 + i].astype(F32) + y_in[i].astype(F32)
+        for l in range(local):
+            out[l] = g[:, l * ff : (l + 1) * ff].astype(BF16)
+
+    for i in range(3):
+        to_core(0, i).wait_send()
+        to_core(1, i).wait_send()
+        to_y(i).wait_send()
+
+    def drain(zz, carry):
+        i = zz * 2 + x
+        for p in pairs:
+
+            @pl.when((zz <= z) & (z < depth - 1))
+            def _():
+                up(p, i).wait_send()
+
+            @pl.when((zz >= z) & (z > 0))
+            def _():
+                down(p, i).wait_send()
+
+            across(p, i).wait_send()
+        share(zz).wait_send()
+
+        @pl.when(zz != z)
+        def _():
+            home(zz).wait_send()
+
+        return carry
+
+    lax.fori_loop(0, depth, drain, 0)
+
+
+def fused(tokens, cotangent, routes, route_weight, w_gate, w_up, w_down):
+    rows, width = tokens.shape
+    local, _, ff = w_gate.shape
+    groups = lax.axis_size("expert")
+    depth = groups // 2
+    wide = local * ff
+    slab = width // lax.axis_size("dp")
+    every = rows * groups
+    full = width + 128
+    vmem = pl.BlockSpec(memory_space=pltpu.VMEM)
+    hbm = pl.BlockSpec(memory_space=pl.ANY)
+    dma = pltpu.SemaphoreType.DMA
+    grad = jax.ShapeDtypeStruct((local, slab, ff), BF16)
+    return pl.pallas_call(
+        functools.partial(kernel, depth),
+        out_shape=(
+            jax.ShapeDtypeStruct(tokens.shape, BF16),
+            jax.ShapeDtypeStruct(routes.shape, BF16),
+            grad,
+            grad,
+            grad,
+        ),
+        in_specs=[vmem] * 4 + [hbm] * 3,
+        out_specs=[vmem] * 5,
+        scratch_shapes=[
+            pltpu.VMEM((every, full), BF16),
+            pltpu.VMEM((every, width), BF16),
+            pltpu.VMEM((width, wide), BF16),
+            pltpu.VMEM((width, wide), BF16),
+            pltpu.VMEM((width, wide), BF16),
+            pltpu.VMEM((every, wide), BF16),
+            pltpu.VMEM((every, wide), BF16),
+            pltpu.VMEM((every, wide), BF16),
+            pltpu.VMEM((every, full), BF16),
+            pltpu.VMEM((depth * rows, full), BF16),
+            pltpu.VMEM((depth * rows, full), BF16),
+            pltpu.VMEM((depth * rows, full), BF16),
+            pltpu.VMEM((6, slab, wide), BF16),
+            pltpu.VMEM((6, slab, wide), BF16),
+            pltpu.VMEM((3, slab, wide), BF16),
+            pltpu.VMEM((3, slab, wide), BF16),
+            pltpu.VMEM((3, slab, wide), F32),
+            dma((3 * local,)),
+            dma((3 * groups,)),
+            dma((3 * groups,)),
+            dma((groups,)),
+            dma((groups,)),
+            dma((depth,)),
+            dma((depth,)),
+            dma((depth,)),
+            dma((depth,)),
+            dma((6,)),
+            dma((6,)),
+            dma((3,)),
+            dma((3,)),
+        ],
+        compiler_params=pltpu.CompilerParams(
+            collective_id=0, has_side_effects=True, vmem_limit_bytes=52 * 1024 * 1024
+        ),
+        cost_estimate=pl.CostEstimate(
+            flops=16 * every * width * wide,
+            bytes_accessed=6 * width * wide,
+            transcendentals=every * wide,
+        ),
+    )(tokens, cotangent, routes, route_weight, w_gate, w_up, w_down)
+
+
 def solution(mesh):
+    small = mesh.shape["expert"] == 8 and mesh.shape["dp"] == 4
     return jax.shard_map(
-        body,
+        fused if small else body,
         mesh=mesh,
         in_specs=(P(("dp", "expert"), None),) * 4 + (P("expert", None, None),) * 3,
         out_specs=(P(("dp", "expert"), None),) * 2 + (P("expert", "dp", None),) * 3,

time: 311 us -> 117 us (0.38)
  waiting for transfers between devices: 232 us -> 0 us
  Pallas kernels: 0 us -> 109 us
  matrix products: 33.5 us -> 0 us
  between operations: 14.4 us -> 0.66 us
  blocking collectives: 8.82 us -> 0 us
  other arithmetic: 8.73 us -> 0 us
  starting transfers between devices: 3.74 us -> 0 us
    reduce_scatter x4 -> x0, waiting for transfers between devices: 130 us -> none  [the longest x1 70.3 us: body(): lax.psum_scatter(grad_rows.astype(jnp.bfloat16), 'expert', scatter_dimens...]
    pallas_call x0 -> x1, Pallas kernels: none -> 109 us  [fused(): pl.pallas_call(functools.partial(kernel, depth), out_shape=(jax.ShapeDtyp...]
    all_gather x2 -> x0, waiting for transfers between devices: 94.7 us -> none  [the longest x1 53.5 us: body(): x = lax.all_gather(tokens, 'expert', tiled=True)]
    dot_general x16 -> x0, matrix products: 33.5 us -> none  [dot(): lax.dot_general(a, b, (dims, ((), ())), preferred_element_type=jnp.float32)]
    all_to_all x1 -> x0, blocking collectives: 8.82 us -> none  [body(): lax.all_to_all(dense.reshape(rows, groups, local).transpose(1, 0, 2), 'ex...]
    all_to_all x1 -> x0, waiting for transfers between devices: 6.25 us -> none  [body(): lax.all_to_all(score.reshape(groups, rows, local), 'expert', 0, 0, tiled=...]
    convert_element_type x4 -> x0, other arithmetic: 4.23 us -> none  [the longest x2 4.22 us: body(): du = (wq * silu).astype(jnp.bfloat16)]
    another operation x4 -> x0, other arithmetic: 3.88 us -> none  [the longest x3 3.87 us: over_dp(): jnp.stack(parts).astype(jnp.bfloat16)]
  transfers between devices with their start and end apart: 7 -> 0, of which waited for: 7 -> 0; matrix products, arithmetic and copies ran while one was open for 11% -> 0% of each run, Pallas kernels for 0% -> 0%
where the time goes in v2:
time: 117 us
  Pallas kernels  109 us (93%)
  local copies, waits for them, and re-layouts  7.08 us (6%)
    pallas_call x1, Pallas kernels, fused(): pl.pallas_call(functools.partial(kernel, depth), out_shape=(jax.ShapeDtyp...  109 us
    unnamed x12, local copies, waits for them, and re-layouts  6.43 us

profile of v2, /device:TPU:0, one launch (start us, length us, event | category | flops | bytes accessed | tf_op | source)
XLA Modules:
  0.0 117.2 jit_solution(3860579493582437896)
XLA Ops:
  0.6 0.8 copy.13.route_weight
  1.4 0.8 copy.12.routes
  2.2 0.0 copy-start
  2.2 0.9 copy-done
  3.2 0.0 copy-start.1
  3.2 0.9 copy-done.1
  4.1 109.5 %shard_map.110 = (bf16[128,1024]{1,0:T(8,128)(2,1)S(1)}, bf16[128,8]{1,0:T(8,128)(2,1)S(1)}, bf16[2,256,384]{2,1,0:T(8,128)(2,1)S(1)}, bf16[2,256,384]{2,1,0:T(8,128)(2,1)S(1)}, bf16[2,256,384]{2,1,0:T(8,128)(2,1)}) custom-call(bf16[128,1024]{1,0:T(8,128)(2,1)S(1)} %copy-done, bf16[128,1024]{1,0:T(8,128)(2,1)S(1)} %copy-done.1, s32[128,8]{1,0:T(8,128)S(1)} %copy.12.routes, ...), custom_call_target="tpu_custom_call" | custom-call | flops 12884901888 | bytes 4718592 | tf_op jit(solution)/shard_map/pallas_call | solution.py:431
  113.6 0.0 copy-start.2
  113.6 0.7 copy.14
  114.3 0.7 copy.19
  115.0 0.7 copy.20
  115.7 0.7 copy.21
  116.5 0.0 copy-done.2
  116.5 0.7 copy.22
Async XLA Ops:
  2.2 0.9 copy-start
  3.2 0.9 copy-start.1
  113.6 2.9 %copy-start.2 = (bf16[2,256,384]{2,1,0:T(8,128)(2,1)S(1)}, bf16[2,256,384]{2,1,0:T(8,128)(2,1)}, u32[]{:S(2)}) copy-start(bf16[2,256,384]{2,1,0:T(8,128)(2,1)} %get-tuple-element.19) | copy-start | bytes 1179652

commit v3 on v2

--- a/solution.py
+++ b/solution.py
@@ -129,7 +129,7 @@
 ):
     rows, width = tokens.shape
     local, _, ff = w_gate.shape
-    top = routes.shape[1]
+    top = routes.shape[0]
     wide = local * ff
     full = width + 128
     slab = out_gate.shape[1]
@@ -163,48 +163,61 @@
     def block(i, n=rows):
         return pl.ds(pl.multiple_of(i * n, n), n)
 
-    lane = lax.broadcasted_iota(jnp.int32, (rows, 128), 1)
-    dense = jnp.zeros((rows, 128), F32)
+    expert = lax.broadcasted_iota(jnp.int32, (128, rows), 0)
+    dense = jnp.zeros((128, rows), F32)
     weights = route_weight[...].astype(F32)
     for k in range(top):
-        dense = dense + jnp.where(routes[:, k : k + 1] == lane, weights[:, k : k + 1], 0.0)
+        dense = dense + jnp.where(routes[k : k + 1, :] == expert, weights[k : k + 1, :], 0.0)
+    dense = dense.T
     xg[block(e), pl.ds(0, width)] = tokens[...]
     xg[block(e), pl.ds(width, 128)] = dense.astype(BF16)
     gg[block(e), :] = cotangent[...]
     pl.semaphore_wait(barrier, depth + 2)
 
-    def move(buf, send, recv, i, way, target):
+    early = 3 * rows // 8
+    pieces = (
+        (xg, send_x, recv_x, 0, 0, early),
+        (xg, send_x, recv_x, 1, early, rows - early),
+        (gg, send_g, recv_g, 0, 0, rows // 2),
+        (gg, send_g, recv_g, 1, rows // 2, rows // 2),
+    )
+
+    def move(piece, i, way, target):
+        buf, send, recv, k, first, count = piece
+        where = pl.ds(pl.multiple_of(i * rows + first, 16), count)
         return pltpu.make_async_remote_copy(
-            buf.at[block(i)],
-            buf.at[block(i)],
-            send.at[i * 3 + way],
-            recv.at[i],
+            buf.at[where],
+            buf.at[where],
+            send.at[(i * 2 + k) * 3 + way],
+            recv.at[i * 2 + k],
             device_id={"expert": target},
             device_id_type=pl.DeviceIdType.MESH,
         )
 
-    pairs = ((xg, send_x, recv_x), (gg, send_g, recv_g))
-
     def up(p, i):
-        return move(*p, i, UP, e + 2)
+        return move(p, i, UP, e + 2)
 
     def down(p, i):
-        return move(*p, i, DOWN, e - 2)
+        return move(p, i, DOWN, e - 2)
 
     def across(p, i):
-        return move(*p, i, ACROSS, partner)
-
-    for p in pairs:
-
+        return move(p, i, ACROSS, partner)
+
+    def along(p, i):
         @pl.when(z < depth - 1)
         def _():
-            up(p, e).start()
+            up(p, i).start()
 
         @pl.when(z > 0)
         def _():
-            down(p, e).start()
-
+            down(p, i).start()
+
+    for p in pieces:
         across(p, e).start()
+        along(p, e)
+        if p is pieces[1]:
+            across(pieces[0], partner).wait_recv()
+            along(pieces[0], partner)
     for c in loads:
         c.wait()
 
@@ -287,39 +300,43 @@
     def step(s, carry):
         d = s + 1
 
-        @pl.when(z - d >= 0)
-        def _():
-            i = e - 2 * d
-            for p in pairs:
+        def pass_on(p, i, below):
+            if below:
                 up(p, i).wait_recv()
 
                 @pl.when(z < depth - 1)
                 def _():
                     up(p, i).start()
 
-                across(p, i).start()
-
-        @pl.when(z + d < depth)
-        def _():
-            i = e + 2 * d
-            for p in pairs:
+            else:
                 down(p, i).wait_recv()
 
                 @pl.when(z > 0)
                 def _():
                     down(p, i).start()
 
-                across(p, i).start()
+        for p in pieces:
+
+            @pl.when(z - d >= 0)
+            def _():
+                pass_on(p, e - 2 * d, True)
+                if p is pieces[0]:
+                    pass_on(p, partner - 2 * d, True)
+                else:
+                    across(p, e - 2 * d).start()
+
+            @pl.when(z + d < depth)
+            def _():
+                pass_on(p, e + 2 * d, False)
+                if p is pieces[0]:
+                    pass_on(p, partner + 2 * d, False)
+                else:
+                    across(p, e + 2 * d).start()
 
         zz = visit(z, s, depth)
-        for p in pairs:
+        for p in pieces[1:]:
             across(p, zz * 2 + 1 - x).wait_recv()
         work(zz)
-        share(zz).start()
-
-        @pl.when(s > 0)
-        def _():
-            reduce(visit(z, s - 1, depth))
 
         return carry
 
@@ -353,20 +370,28 @@
             device_id_type=pl.DeviceIdType.MESH,
         )
 
+    def ahead(k):
+        return visit(z, depth - 1 - k, depth)
+
+    for k in range(depth):
+        share(ahead(k)).start()
     for i, g in enumerate(slab_grads((1 - y) * 2 + 1 - core)):
         core_out[i] = g.astype(BF16)
         to_core(0, i).start()
-    reduce(visit(z, depth - 1, depth))
     for i, g in enumerate(slab_grads(y_peer)):
         acc[i] = g
         to_core(0, i).wait_recv()
         y_out[i] = (acc[i] + core_in[i].astype(F32)).astype(BF16)
         to_y(i).start()
+    reduce(ahead(0))
     for i, g in enumerate(slab_grads(core_peer)):
         core_out[3 + i] = g.astype(BF16)
         to_core(1, i).start()
+    reduce(ahead(1))
     for i, g in enumerate(slab_grads(dp)):
         acc[i] = g
+    for k in range(2, depth):
+        reduce(ahead(k))
 
     total = red[block(z), :].astype(F32)
     for k in range(1, depth):
@@ -374,10 +399,12 @@
         landed(zz).wait_recv()
         total = total + red_in[block(zz), :].astype(F32)
     out_tokens[...] = total[:, :width].astype(BF16)
-    scores = total[:, width:full]
+    scores = total[:, width:full].T
+    picked = []
     for k in range(top):
-        mine = jnp.where(routes[:, k : k + 1] == lane, scores, 0.0)
-        out_weight[:, k : k + 1] = jnp.sum(mine, axis=1, keepdims=True).astype(BF16)
+        mine = jnp.where(routes[k : k + 1, :] == expert, scores, 0.0)
+        picked.append(jnp.sum(mine, axis=0, keepdims=True))
+    out_weight[...] = jnp.concatenate(picked, axis=0).astype(BF16)
 
     for i, out in enumerate((out_gate, out_up, out_down)):
         to_core(1, i).wait_recv()
@@ -386,6 +413,7 @@
         for l in range(local):
             out[l] = g[:, l * ff : (l + 1) * ff].astype(BF16)
 
+    across(pieces[0], e).wait_send()
     for i in range(3):
         to_core(0, i).wait_send()
         to_core(1, i).wait_send()
@@ -393,8 +421,7 @@
 
     def drain(zz, carry):
         i = zz * 2 + x
-        for p in pairs:
-
+        def sent(p, i):
             @pl.when((zz <= z) & (z < depth - 1))
             def _():
                 up(p, i).wait_send()
@@ -403,6 +430,10 @@
             def _():
                 down(p, i).wait_send()
 
+        for p in pieces:
+            sent(p, i)
+        sent(pieces[0], zz * 2 + 1 - x)
+        for p in pieces[1:]:
             across(p, i).wait_send()
         share(zz).wait_send()
 
@@ -428,11 +459,11 @@
     hbm = pl.BlockSpec(memory_space=pl.ANY)
     dma = pltpu.SemaphoreType.DMA
     grad = jax.ShapeDtypeStruct((local, slab, ff), BF16)
-    return pl.pallas_call(
+    outs = pl.pallas_call(
         functools.partial(kernel, depth),
         out_shape=(
             jax.ShapeDtypeStruct(tokens.shape, BF16),
-            jax.ShapeDtypeStruct(routes.shape, BF16),
+            jax.ShapeDtypeStruct(routes.shape[::-1], BF16),
             grad,
             grad,
             grad,
@@ -458,10 +489,10 @@
             pltpu.VMEM((3, slab, wide), BF16),
             pltpu.VMEM((3, slab, wide), F32),
             dma((3 * local,)),
-            dma((3 * groups,)),
-            dma((3 * groups,)),
-            dma((groups,)),
-            dma((groups,)),
+            dma((6 * groups,)),
+            dma((6 * groups,)),
+            dma((2 * groups,)),
+            dma((2 * groups,)),
             dma((depth,)),
             dma((depth,)),
             dma((depth,)),
@@ -479,7 +510,8 @@
             bytes_accessed=6 * width * wide,
             transcendentals=every * wide,
         ),
-    )(tokens, cotangent, routes, route_weight, w_gate, w_up, w_down)
+    )(tokens, cotangent, routes.T, route_weight.T, w_gate, w_up, w_down)
+    return outs[0], outs[1].T, *outs[2:]
 
 
 def solution(mesh):

time: 117 us -> 97.7 us (0.84)
  Pallas kernels: 109 us -> 90 us
    pallas_call x1, Pallas kernels: 109 us -> 90 us  [fused(): pl.pallas_call(functools.partial(kernel, depth), out_shape=(jax.ShapeDtyp...]
    unnamed x12 -> x13, local copies, waits for them, and re-layouts: 6.43 us -> 6.78 us
where the time goes in v3:
time: 97.7 us; the launch traced here: 97.5 us
  Pallas kernels  90 us (92%)
  local copies, waits for them, and re-layouts  6.78 us (7%)
    pallas_call x1, Pallas kernels, fused(): pl.pallas_call(functools.partial(kernel, depth), out_shape=(jax.ShapeDtyp...  90 us
    unnamed x13, local copies, waits for them, and re-layouts  6.78 us

profile of v3, /device:TPU:0, one launch (start us, length us, event | category | flops | bytes accessed | tf_op | source)
XLA Modules:
  0.0 97.5 jit_solution(13691587641890451675)
XLA Ops:
  0.6 0.0 copy-start
  0.6 0.9 copy-done
  1.6 0.0 copy-start.1
  1.6 0.9 copy-done.1
  2.5 0.0 copy-start.2
  2.5 0.7 copy-done.2
  3.2 0.0 copy-start.3
  3.2 0.7 copy-done.3
  3.9 90.0 %shard_map.110 = (bf16[128,1024]{1,0:T(8,128)(2,1)S(1)}, bf16[8,128]{1,0:T(8,128)(2,1)S(1)}, bf16[2,256,384]{2,1,0:T(8,128)(2,1)S(1)}, bf16[2,256,384]{2,1,0:T(8,128)(2,1)S(1)}, bf16[2,256,384]{2,1,0:T(8,128)(2,1)S(1)}) custom-call(bf16[128,1024]{1,0:T(8,128)(2,1)S(1)} %copy-done, bf16[128,1024]{1,0:T(8,128)(2,1)S(1)} %copy-done.1, s32[8,128]{1,0:T(8,128)S(1)} %bitcast.4, ...), custom_call_target="tpu_custom_call" | custom-call | flops 12884901888 | bytes 4718592 | tf_op jit(solution)/shard_map/pallas_call | solution.py:462
  93.9 0.7 copy.17
  94.7 0.6 copy.18
  95.2 0.7 copy.19
  96.0 0.7 copy.20
  96.7 0.7 copy.21
Async XLA Ops:
  0.6 1.0 copy-start
  1.6 0.9 copy-start.1
  2.5 0.7 copy-start.2
  3.2 0.7 copy-start.3

commit v4 on v3

--- a/solution.py
+++ b/solution.py
@@ -174,7 +174,7 @@
     gg[block(e), :] = cotangent[...]
     pl.semaphore_wait(barrier, depth + 2)
 
-    early = 3 * rows // 8
+    early = rows // 2
     pieces = (
         (xg, send_x, recv_x, 0, 0, early),
         (xg, send_x, recv_x, 1, early, rows - early),
@@ -338,6 +338,10 @@
             across(p, zz * 2 + 1 - x).wait_recv()
         work(zz)
 
+        @pl.when(s == 0)
+        def _():
+            share(zz).start()
+
         return carry
 
     lax.fori_loop(0, depth, step, 0)
@@ -373,7 +377,7 @@
     def ahead(k):
         return visit(z, depth - 1 - k, depth)
 
-    for k in range(depth):
+    for k in range(depth - 1):
         share(ahead(k)).start()
     for i, g in enumerate(slab_grads((1 - y) * 2 + 1 - core)):
         core_out[i] = g.astype(BF16)

time: 97.7 us -> 99.7 us (1.020)
  Pallas kernels: 90 us -> 92 us
    pallas_call x1, Pallas kernels: 90 us -> 92 us  [fused(): pl.pallas_call(functools.partial(kernel, depth), out_shape=(jax.ShapeDtyp...]
where the time goes in v4:
time: 99.7 us; the launch traced here: 99.4 us
  Pallas kernels  92 us (92%)
  local copies, waits for them, and re-layouts  6.78 us (7%)
    pallas_call x1, Pallas kernels, fused(): pl.pallas_call(functools.partial(kernel, depth), out_shape=(jax.ShapeDtyp...  92 us
    unnamed x13, local copies, waits for them, and re-layouts  6.78 us

profile of v4, /device:TPU:0, one launch (start us, length us, event | category | flops | bytes accessed | tf_op | source)
XLA Modules:
  0.0 99.4 jit_solution(3654745362122203045)
XLA Ops:
  0.6 0.0 copy-start
  0.6 0.9 copy-done
  1.6 0.0 copy-start.1
  1.6 0.9 copy-done.1
  2.5 0.0 copy-start.2
  2.5 0.7 copy-done.2
  3.2 0.0 copy-start.3
  3.2 0.7 copy-done.3
  3.9 92.0 %shard_map.110 = (bf16[128,1024]{1,0:T(8,128)(2,1)S(1)}, bf16[8,128]{1,0:T(8,128)(2,1)S(1)}, bf16[2,256,384]{2,1,0:T(8,128)(2,1)S(1)}, bf16[2,256,384]{2,1,0:T(8,128)(2,1)S(1)}, bf16[2,256,384]{2,1,0:T(8,128)(2,1)S(1)}) custom-call(bf16[128,1024]{1,0:T(8,128)(2,1)S(1)} %copy-done, bf16[128,1024]{1,0:T(8,128)(2,1)S(1)} %copy-done.1, s32[8,128]{1,0:T(8,128)S(1)} %bitcast.4, ...), custom_call_target="tpu_custom_call" | custom-call | flops 12884901888 | bytes 4718592 | tf_op jit(solution)/shard_map/pallas_call | solution.py:466
  95.9 0.7 copy.17
  96.6 0.6 copy.18
  97.2 0.7 copy.19
  97.9 0.7 copy.20
  98.7 0.7 copy.21
Async XLA Ops:
  0.6 1.0 copy-start
  1.6 0.9 copy-start.1
  2.5 0.7 copy-start.2
  3.2 0.7 copy-start.3
